TPU v7x, 512 devices: a whole 4x4x16 slice. The times are simulated.
512 devices in a mesh: arm: 8 (over x_lo, y), sx: 32 (over z, core), sy: 2 (over x_hi).
Axes of the slice: x: 4 (x_hi: 2, x_lo: 2; x = x_hi * 2 + x_lo), y: 4, z: 16, core: 2. Of those that a mesh axis runs over, the one named last changes fastest.
Arguments:
- forward_end: float32 [16, 128, 256, 256], P('arm', 'sx', 'sy'), may hold values from 0.5 to 2
- partner_end: float32 [16, 128, 256, 256], P('arm', 'sx', 'sy'), may hold values from 0.5 to 2
- potential: float32 [2, 128, 256, 256], P(None, 'sx', 'sy'), may hold values from -3 to 3
- species_label: int32 [16], P('arm'), may hold values from 0 to 1
- arm_length: int32 [16], P('arm'), may hold values from 1 to 3, as said below
Outputs:
- conjugate: float32 [16, 128, 256, 256], P('arm', 'sx', 'sy')
- density: float32 [2, 128, 256, 256], P(None, 'sx', 'sy')
Inputs may be any that keep to these rules, and one draw needn't show every extreme that they name: `arm_length`: some arm has exactly 3 steps in every draw.
All inputs are finite; a program needn't handle non-finite values.
Results may differ from a plain program's by a relative error of at most 0.000036.
Values sent between devices are 32-bit elements; how exact they have to be, the bound alone decides.
A program may use at most 64 MiB of HBM per device.

v0:
```python
import jax
import jax.numpy as jnp
from jax import lax
from jax.sharding import PartitionSpec as P

MAXSTEPS = 3


STIFF = 0.16


def extended(value, sides, width):
    for axis, dim in sides:
        count, length = (lax.axis_size(axis), value.shape[dim])
        up = [(i, (i + 1) % count) for i in range(count)]
        down = [(j, i) for i, j in up]
        last = lax.slice_in_dim(value, length - width, length, axis=dim)
        first = lax.slice_in_dim(value, 0, width, axis=dim)
        before = lax.ppermute(last, axis, up)
        after = lax.ppermute(first, axis, down)
        value = jnp.concatenate([before, value, after], axis=dim)
    return value


def interior(padded, inner_part):
    laplace = (
        padded[:, 2:, 1:-1] + padded[:, :-2, 1:-1] + padded[:, 1:-1, 2:] + padded[:, 1:-1, :-2]
    )
    laplace = laplace + jnp.roll(inner_part, 1, 3) + jnp.roll(inner_part, -1, 3) - 6.0 * inner_part
    return inner_part + STIFF * laplace


def single_step(field, factor):
    inner = factor * field
    padded = extended(inner, (("sx", 1), ("sy", 2)), 1)
    return factor * interior(padded, inner)


def local(forward_end, partner_end, potential, species_label, arm_length):
    logs = jnp.log(forward_end)
    logsum = lax.psum(jnp.sum(logs, axis=0), "arm")
    current = jnp.exp(logsum[None] - logs)
    factor = jnp.exp(
        -0.5
        * jnp.where(
            (species_label == 1)[:, None, None, None], potential[1][None], potential[0][None]
        )
    )
    lengths = arm_length[:, None, None, None]

    def advance(step_index, field):
        updated = single_step(field, factor)
        return jnp.where(lengths > step_index, updated, field)

    current = lax.fori_loop(0, MAXSTEPS, advance, current)
    product = partner_end * current
    dens_zero = jnp.sum(jnp.where((species_label == 0)[:, None, None, None], product, 0.0), axis=0)
    dens_one = jnp.sum(jnp.where((species_label == 1)[:, None, None, None], product, 0.0), axis=0)
    density = lax.psum(jnp.stack([dens_zero, dens_one]), "arm")
    return (current, density)


def solution(mesh):
    return jax.shard_map(
        local,
        mesh=mesh,
        in_specs=(
            P("arm", "sx", "sy", None),
            P("arm", "sx", "sy", None),
            P(None, "sx", "sy", None),
            P("arm"),
            P("arm"),
        ),
        out_specs=(P("arm", "sx", "sy", None), P(None, "sx", "sy", None)),
        check_vma=False,
    )
```

profile of v0, /device:TPU:4, one launch (start us, length us, event | category | flops | bytes accessed | tf_op | source)
XLA Modules:
  0.0 281.4 jit_solution(13619236405384795670)
XLA Ops:
  7.2 2.3 log_reduce_fusion
  11.2 94.7 %all-reduce.3.cloned.1.call-done = f32[4,128,256]{2,1,0:T(8,128)} async-done(((f32[4,128,256]{2,1,0:T(8,128)}), f32[4,128,256]{2,1,0:T(8,128)}) %all-reduce.3.cloned.1.call-update) | async-done | bytes 524304 | tf_op jit(solution)/shard_map/psum | solution.py:41
  107.9 69.9 %while.14 = (s32[]{:T(128)}, f32[2,4,128,256]{3,2,1,0:T(8,128)S(1)}, s32[2,1,1,1]{0,3,2,1:T(1,128)S(1)}, f32[4,128,256]{2,1,0:T(8,128)}, f32[4,128,256]{2,1,0:T(8,128)}, /*index=5*/pred[2]{0:T(512)(128)(4,1)S(1)}, s32[]{:T(128)}) while((s32[]{:T(128)}, f32[2,4,128,256]{3,2,1,0:T(8,128)S(1)}, s32[2,1,1,1]{0,3,2,1:T(1,128)S(1)}, ...), condition=%wide.region_3.4_spmd.clone, body=%wide.region_2.3_spmd.clone.sunk | while | flops 6828036 | bytes 20070684 | solution.py:55
  107.9 1.4 fusion.21
  113.3 4.3 %collective-permute-done.1 = f32[2,1,128,256]{3,2,1,0:T(8,128)S(1)} collective-permute-done((f32[2,1,128,256]{3,2,1,0:T(8,128)S(1)}, f32[2,1,128,256]{3,2,1,0:T(8,128)S(1)}, u32[]{:S(2)}, u32[]{:S(2)}) %collective-permute-start.1) | collective-permute-done | bytes 262176 | tf_op jit(solution)/shard_map/while/body/eval_jaxpr/ppermute | solution.py:19
  118.3 2.7 collective-permute-start.2
  121.1 4.6 %collective-permute-start.3 = (f32[2,6,1,256]{3,2,1,0:T(1,128)S(1)}, f32[2,6,1,256]{3,2,1,0:T(1,128)S(1)}, u32[]{:S(2)}, u32[]{:S(2)}) collective-permute-start(f32[2,6,1,256]{3,2,1,0:T(1,128)S(1)} %get-tuple-element.173), channel_id=1, source_target_pairs={{1,0},{0,1},{3,2},{2,3},{5,4},{4,5},{7,6},{6,7},{9,8},{8,9},{11,10... | collective-permute-start | bytes 36872 | tf_op jit(solution)/shard_map/while/body/eval_jaxpr/ppermute | solution.py:20
  125.7 2.5 collective-permute-done.3
  128.1 3.2 %fusion.25 = f32[2,4,128,256]{3,2,1,0:T(8,128)S(1)} fusion(f32[2,4,128,256]{3,2,1,0:T(8,128)S(1)} %get-tuple-element.186, f32[2,4,128,256]{3,2,1,0:T(8,128)S(1)} %fusion.21, f32[2,6,1,256]{3,2,1,0:T(1,128)S(1)} %collective-permute-done.2, f32[2,1,128,256]{3,2,1,0:T(8,128)S(1)} %collective-permute-done, f32[2,1,128,256]{3,2,1,0:T(8,128)} %copy-done.1, ...), kind=kLoop, calls=%fused_computation.9.clone.1 | loop fusion | flops 6029312 | bytes 6840324 | tf_op jit(solution)/shard_map/while/body/eval_jaxpr/jit(_where)/select_n | solution.py:53
  131.4 1.4 fusion.21
  136.8 3.1 %collective-permute-done.1 = f32[2,1,128,256]{3,2,1,0:T(8,128)S(1)} collective-permute-done((f32[2,1,128,256]{3,2,1,0:T(8,128)S(1)}, f32[2,1,128,256]{3,2,1,0:T(8,128)S(1)}, u32[]{:S(2)}, u32[]{:S(2)}) %collective-permute-start.1) | collective-permute-done | bytes 262176 | tf_op jit(solution)/shard_map/while/body/eval_jaxpr/ppermute | solution.py:19
  140.6 4.6 %collective-permute-start.2 = (f32[2,6,1,256]{3,2,1,0:T(1,128)S(1)}, f32[2,6,1,256]{3,2,1,0:T(1,128)S(1)}, u32[]{:S(2)}, u32[]{:S(2)}) collective-permute-start(f32[2,6,1,256]{3,2,1,0:T(1,128)S(1)} %get-tuple-element.172), channel_id=1, source_target_pairs={{0,1},{1,0},{2,3},{3,2},{4,5},{5,4},{6,7},{7,6},{8,9},{9,8},{10,11... | collective-permute-start | bytes 36872 | tf_op jit(solution)/shard_map/while/body/eval_jaxpr/ppermute | solution.py:19
  145.2 2.8 collective-permute-start.3
  148.0 4.3 %collective-permute-done.3 = f32[2,6,1,256]{3,2,1,0:T(1,128)S(1)} collective-permute-done((f32[2,6,1,256]{3,2,1,0:T(1,128)S(1)}, f32[2,6,1,256]{3,2,1,0:T(1,128)S(1)}, u32[]{:S(2)}, u32[]{:S(2)}) %collective-permute-start.3) | collective-permute-done | bytes 12320 | tf_op jit(solution)/shard_map/while/body/eval_jaxpr/ppermute | solution.py:20
  152.3 3.2 %fusion.25 = f32[2,4,128,256]{3,2,1,0:T(8,128)S(1)} fusion(f32[2,4,128,256]{3,2,1,0:T(8,128)S(1)} %get-tuple-element.186, f32[2,4,128,256]{3,2,1,0:T(8,128)S(1)} %fusion.21, f32[2,6,1,256]{3,2,1,0:T(1,128)S(1)} %collective-permute-done.2, f32[2,1,128,256]{3,2,1,0:T(8,128)S(1)} %collective-permute-done, f32[2,1,128,256]{3,2,1,0:T(8,128)} %copy-done.1, ...), kind=kLoop, calls=%fused_computation.9.clone.1 | loop fusion | flops 6029312 | bytes 6840324 | tf_op jit(solution)/shard_map/while/body/eval_jaxpr/jit(_where)/select_n | solution.py:53
  155.5 1.4 fusion.21
  160.9 3.1 %collective-permute-done.1 = f32[2,1,128,256]{3,2,1,0:T(8,128)S(1)} collective-permute-done((f32[2,1,128,256]{3,2,1,0:T(8,128)S(1)}, f32[2,1,128,256]{3,2,1,0:T(8,128)S(1)}, u32[]{:S(2)}, u32[]{:S(2)}) %collective-permute-start.1) | collective-permute-done | bytes 262176 | tf_op jit(solution)/shard_map/while/body/eval_jaxpr/ppermute | solution.py:19
  164.7 2.7 collective-permute-start.2
  167.5 4.6 %collective-permute-start.3 = (f32[2,6,1,256]{3,2,1,0:T(1,128)S(1)}, f32[2,6,1,256]{3,2,1,0:T(1,128)S(1)}, u32[]{:S(2)}, u32[]{:S(2)}) collective-permute-start(f32[2,6,1,256]{3,2,1,0:T(1,128)S(1)} %get-tuple-element.173), channel_id=1, source_target_pairs={{1,0},{0,1},{3,2},{2,3},{5,4},{4,5},{7,6},{6,7},{9,8},{8,9},{11,10... | collective-permute-start | bytes 36872 | tf_op jit(solution)/shard_map/while/body/eval_jaxpr/ppermute | solution.py:20
  172.1 2.5 collective-permute-done.3
  174.6 3.2 %fusion.25 = f32[2,4,128,256]{3,2,1,0:T(8,128)S(1)} fusion(f32[2,4,128,256]{3,2,1,0:T(8,128)S(1)} %get-tuple-element.186, f32[2,4,128,256]{3,2,1,0:T(8,128)S(1)} %fusion.21, f32[2,6,1,256]{3,2,1,0:T(1,128)S(1)} %collective-permute-done.2, f32[2,1,128,256]{3,2,1,0:T(8,128)S(1)} %collective-permute-done, f32[2,1,128,256]{3,2,1,0:T(8,128)} %copy-done.1, ...), kind=kLoop, calls=%fused_computation.9.clone.1 | loop fusion | flops 6029312 | bytes 6840324 | tf_op jit(solution)/shard_map/while/body/eval_jaxpr/jit(_where)/select_n | solution.py:53
  177.8 2.0 select_reduce_fusion.1
  180.9 91.4 %all-reduce.5.cloned.1.call-done = f32[2,4,128,256]{3,2,1,0:T(8,128)} async-done(((f32[2,4,128,256]{3,2,1,0:T(8,128)}), f32[2,4,128,256]{3,2,1,0:T(8,128)}) %all-reduce.5.cloned.1.call-update) | async-done | bytes 1048592 | tf_op jit(solution)/shard_map/psum | solution.py:59
  272.3 2.3 copy.17
  (51 shorter events, 18.7 us)
Async XLA Ops:
  7.2 3.0 %copy-start.3 = (f32[2,4,128,256]{3,2,1,0:T(8,128)S(1)}, f32[2,4,128,256]{3,2,1,0:T(8,128)}, u32[]{:S(2)}) copy-start(f32[2,4,128,256]{3,2,1,0:T(8,128)} %param.9) | copy-start | bytes 3145732
  7.2 98.7 %all-reduce.3.cloned.1.call-start = ((), (), s32[]{:S(2)}) async-start(), calls=%async_computation | async-start | bytes 1048576 | tf_op jit(solution)/shard_map/psum | solution.py:41
  9.5 0.7 copy-start.4
  9.5 262.7 %all-reduce.5.cloned.1.call-start = ((), (), s32[]{:S(2)}) async-start(), calls=%async_computation.1 | async-start | bytes 2097152 | tf_op jit(solution)/shard_map/psum | solution.py:59
  10.2 95.7 %copy-start.2 = (f32[2,4,128,256]{3,2,1,0:T(8,128)S(1)}, f32[2,4,128,256]{3,2,1,0:T(8,128)}, u32[]{:S(2)}) copy-start(f32[2,4,128,256]{3,2,1,0:T(8,128)} %param.7) | copy-start | bytes 3145732
  107.2 0.7 copy-start.5
  109.4 3.9 %collective-permute-start = (f32[2,1,128,256]{3,2,1,0:T(8,128)S(1)}, f32[2,1,128,256]{3,2,1,0:T(8,128)S(1)}, u32[]{:S(2)}, u32[]{:S(2)}) collective-permute-start(f32[2,1,128,256]{3,2,1,0:T(8,128)S(1)} %get-tuple-element.170), channel_id=1, source_target_pairs={{2,0},{4,2},{6,4},{8,6},{10,8},{12,10},{14,12},{16,14},{18,16},{20... | collective-permute-start | bytes 786440 | tf_op jit(solution)/shard_map/while/body/eval_jaxpr/ppermute | solution.py:20
  109.4 8.2 %collective-permute-start.1 = (f32[2,1,128,256]{3,2,1,0:T(8,128)S(1)}, f32[2,1,128,256]{3,2,1,0:T(8,128)S(1)}, u32[]{:S(2)}, u32[]{:S(2)}) collective-permute-start(f32[2,1,128,256]{3,2,1,0:T(8,128)S(1)} %get-tuple-element.171), channel_id=1, source_target_pairs={{0,2},{2,4},{4,6},{6,8},{8,10},{10,12},{12,14},{14,16},{16,18},{18... | collective-permute-start | bytes 786440 | tf_op jit(solution)/shard_map/while/body/eval_jaxpr/ppermute | solution.py:19
  117.6 0.7 copy-start.1
  118.3 7.4 %collective-permute-start.2 = (f32[2,6,1,256]{3,2,1,0:T(1,128)S(1)}, f32[2,6,1,256]{3,2,1,0:T(1,128)S(1)}, u32[]{:S(2)}, u32[]{:S(2)}) collective-permute-start(f32[2,6,1,256]{3,2,1,0:T(1,128)S(1)} %get-tuple-element.172), channel_id=1, source_target_pairs={{0,1},{1,0},{2,3},{3,2},{4,5},{5,4},{6,7},{7,6},{8,9},{9,8},{10,11... | collective-permute-start | bytes 36872 | tf_op jit(solution)/shard_map/while/body/eval_jaxpr/ppermute | solution.py:19
  121.1 7.1 %collective-permute-start.3 = (f32[2,6,1,256]{3,2,1,0:T(1,128)S(1)}, f32[2,6,1,256]{3,2,1,0:T(1,128)S(1)}, u32[]{:S(2)}, u32[]{:S(2)}) collective-permute-start(f32[2,6,1,256]{3,2,1,0:T(1,128)S(1)} %get-tuple-element.173), channel_id=1, source_target_pairs={{1,0},{0,1},{3,2},{2,3},{5,4},{4,5},{7,6},{6,7},{9,8},{8,9},{11,10... | collective-permute-start | bytes 36872 | tf_op jit(solution)/shard_map/while/body/eval_jaxpr/ppermute | solution.py:20
  132.9 3.9 %collective-permute-start = (f32[2,1,128,256]{3,2,1,0:T(8,128)S(1)}, f32[2,1,128,256]{3,2,1,0:T(8,128)S(1)}, u32[]{:S(2)}, u32[]{:S(2)}) collective-permute-start(f32[2,1,128,256]{3,2,1,0:T(8,128)S(1)} %get-tuple-element.170), channel_id=1, source_target_pairs={{2,0},{4,2},{6,4},{8,6},{10,8},{12,10},{14,12},{16,14},{18,16},{20... | collective-permute-start | bytes 786440 | tf_op jit(solution)/shard_map/while/body/eval_jaxpr/ppermute | solution.py:20
  132.9 7.0 %collective-permute-start.1 = (f32[2,1,128,256]{3,2,1,0:T(8,128)S(1)}, f32[2,1,128,256]{3,2,1,0:T(8,128)S(1)}, u32[]{:S(2)}, u32[]{:S(2)}) collective-permute-start(f32[2,1,128,256]{3,2,1,0:T(8,128)S(1)} %get-tuple-element.171), channel_id=1, source_target_pairs={{0,2},{2,4},{4,6},{6,8},{8,10},{10,12},{12,14},{14,16},{16,18},{18... | collective-permute-start | bytes 786440 | tf_op jit(solution)/shard_map/while/body/eval_jaxpr/ppermute | solution.py:19
  139.9 0.7 copy-start.1
  140.6 7.4 %collective-permute-start.2 = (f32[2,6,1,256]{3,2,1,0:T(1,128)S(1)}, f32[2,6,1,256]{3,2,1,0:T(1,128)S(1)}, u32[]{:S(2)}, u32[]{:S(2)}) collective-permute-start(f32[2,6,1,256]{3,2,1,0:T(1,128)S(1)} %get-tuple-element.172), channel_id=1, source_target_pairs={{0,1},{1,0},{2,3},{3,2},{4,5},{5,4},{6,7},{7,6},{8,9},{9,8},{10,11... | collective-permute-start | bytes 36872 | tf_op jit(solution)/shard_map/while/body/eval_jaxpr/ppermute | solution.py:19
  145.2 7.1 %collective-permute-start.3 = (f32[2,6,1,256]{3,2,1,0:T(1,128)S(1)}, f32[2,6,1,256]{3,2,1,0:T(1,128)S(1)}, u32[]{:S(2)}, u32[]{:S(2)}) collective-permute-start(f32[2,6,1,256]{3,2,1,0:T(1,128)S(1)} %get-tuple-element.173), channel_id=1, source_target_pairs={{1,0},{0,1},{3,2},{2,3},{5,4},{4,5},{7,6},{6,7},{9,8},{8,9},{11,10... | collective-permute-start | bytes 36872 | tf_op jit(solution)/shard_map/while/body/eval_jaxpr/ppermute | solution.py:20
  157.0 3.9 %collective-permute-start = (f32[2,1,128,256]{3,2,1,0:T(8,128)S(1)}, f32[2,1,128,256]{3,2,1,0:T(8,128)S(1)}, u32[]{:S(2)}, u32[]{:S(2)}) collective-permute-start(f32[2,1,128,256]{3,2,1,0:T(8,128)S(1)} %get-tuple-element.170), channel_id=1, source_target_pairs={{2,0},{4,2},{6,4},{8,6},{10,8},{12,10},{14,12},{16,14},{18,16},{20... | collective-permute-start | bytes 786440 | tf_op jit(solution)/shard_map/while/body/eval_jaxpr/ppermute | solution.py:20
  157.0 7.0 %collective-permute-start.1 = (f32[2,1,128,256]{3,2,1,0:T(8,128)S(1)}, f32[2,1,128,256]{3,2,1,0:T(8,128)S(1)}, u32[]{:S(2)}, u32[]{:S(2)}) collective-permute-start(f32[2,1,128,256]{3,2,1,0:T(8,128)S(1)} %get-tuple-element.171), channel_id=1, source_target_pairs={{0,2},{2,4},{4,6},{6,8},{8,10},{10,12},{12,14},{14,16},{16,18},{18... | collective-permute-start | bytes 786440 | tf_op jit(solution)/shard_map/while/body/eval_jaxpr/ppermute | solution.py:19
  164.0 0.7 copy-start.1
  164.7 7.4 %collective-permute-start.2 = (f32[2,6,1,256]{3,2,1,0:T(1,128)S(1)}, f32[2,6,1,256]{3,2,1,0:T(1,128)S(1)}, u32[]{:S(2)}, u32[]{:S(2)}) collective-permute-start(f32[2,6,1,256]{3,2,1,0:T(1,128)S(1)} %get-tuple-element.172), channel_id=1, source_target_pairs={{0,1},{1,0},{2,3},{3,2},{4,5},{5,4},{6,7},{7,6},{8,9},{9,8},{10,11... | collective-permute-start | bytes 36872 | tf_op jit(solution)/shard_map/while/body/eval_jaxpr/ppermute | solution.py:19
  167.5 7.1 %collective-permute-start.3 = (f32[2,6,1,256]{3,2,1,0:T(1,128)S(1)}, f32[2,6,1,256]{3,2,1,0:T(1,128)S(1)}, u32[]{:S(2)}, u32[]{:S(2)}) collective-permute-start(f32[2,6,1,256]{3,2,1,0:T(1,128)S(1)} %get-tuple-element.173), channel_id=1, source_target_pairs={{1,0},{0,1},{3,2},{2,3},{5,4},{4,5},{7,6},{6,7},{9,8},{8,9},{11,10... | collective-permute-start | bytes 36872 | tf_op jit(solution)/shard_map/while/body/eval_jaxpr/ppermute | solution.py:20
  177.8 2.0 copy-start
Sparse Core Ops, SparseCore 0:
  11.5 94.3 all-reduce.2
  181.0 91.2 all-reduce.4
where the time goes:
time: 282 us; the launch traced here: 281 us
  waiting for transfers between devices  209 us (74%)
  starting transfers between devices  23.6 us (8%)
  other arithmetic  20.6 us (7%)
  local copies, waits for them, and re-layouts  14.1 us (5%)
  between operations  14.1 us (5%)
    psum x1, waiting for transfers between devices, local(): logsum = lax.psum(jnp.sum(logs, axis=0), 'arm')  94.7 us
    psum x1, waiting for transfers between devices, local(): density = lax.psum(jnp.stack([dens_zero, dens_one]), 'arm')  91.4 us
    ppermute x6, waiting for transfers between devices, extended(): after = lax.ppermute(first, axis, down)  12 us
    ppermute x6, starting transfers between devices, extended(): after = lax.ppermute(first, axis, down)  12 us
    ppermute x6, starting transfers between devices, extended(): before = lax.ppermute(last, axis, up)  11.6 us
    ppermute x6, waiting for transfers between devices, extended(): before = lax.ppermute(last, axis, up)  10.6 us
    select_n x3, other arithmetic, advance(): return jnp.where(lengths > step_index, updated, field)  9.55 us
    slice x6, local copies, waits for them, and re-layouts, interior(): jnp.roll(inner_part, -1, 3)  7.37 us
  transfers between devices with their start and end apart: 14, of which 11 were waited for; matrix products, arithmetic and copies ran while one was open for 3% of the time, Pallas kernels for 0%

commit v1 on v0

v1 whole, which is shorter than its diff:
```python
import jax
import jax.numpy as jnp
from jax import lax
from jax.experimental import pallas as pl
from jax.experimental.pallas import tpu as pltpu
from jax.sharding import PartitionSpec as P

MESH = pl.DeviceIdType.MESH
F32 = jnp.float32
ROWS, NYL, LANES = 4, 128, 128
YD, Y0 = 160, 16
BLK = 24


def kernel(
    lab, length, fwd, par, pot, conj, dens,
    fv, pv, uv, p, prx, pext, c, ifac, va, vb, cj, dp, drx, do,
    lsem, bsend, brecv, psend, precv, hsend, hrecv, dsend, drecv,
):
    arm, sx, sy = lax.axis_index("arm"), lax.axis_index("sx"), lax.axis_index("sy")
    x, y = arm // 4, arm % 4
    xs = [x, 1 - x]
    ys = [y, y + 1 - 2 * (y % 2), (y + 2) % 4, 3 - y]
    peers = [(xs[d // 4], ys[d % 4]) for d in range(8)]
    up, down, other = (sx + 1) % 32, (sx + 31) % 32, 1 - sy

    def arm_dev(d):
        return {"arm": peers[d][0] * 4 + peers[d][1]}

    around = [{"sx": up}, {"sx": down}, {"sy": other}, {"sx": up, "sy": other}, {"sx": down, "sy": other}]

    loads = []

    def load(src, dst):
        cp = pltpu.make_async_copy(src, dst, lsem.at[len(loads)])
        cp.start()
        loads.append(cp)

    for src, dst in ((fwd, fv), (pot, uv), (par, pv)):
        for h in range(2):
            load(src.at[:, :, :, pl.ds(h * LANES, LANES)], dst.at[:, :, h])

    barrier = pltpu.get_barrier_semaphore()
    for d in range(1, 8):
        pl.semaphore_signal(barrier, inc=1, device_id=arm_dev(d), device_id_type=MESH)
    for dev in around:
        pl.semaphore_signal(barrier, inc=1, device_id=dev, device_id_type=MESH)

    loads[0].wait()
    loads[1].wait()

    @pl.loop(0, ROWS)
    def _(r):
        for h in range(2):
            p[r, h] = fv[0, r, h] * fv[1, r, h]

    pl.semaphore_wait(barrier, 12)

    def send(src, dst, ssem, rsem, dev):
        cp = pltpu.make_async_remote_copy(
            src_ref=src, dst_ref=dst, send_sem=ssem, recv_sem=rsem, device_id=dev, device_id_type=MESH
        )
        cp.start()
        return cp

    sent = []
    rs = []
    for d in range(1, 8):
        px, py = peers[d]
        rs.append(send(p.at[py, px], prx.at[d], psend.at[d], precv.at[d], arm_dev(d)))
    sent += rs

    loads[2].wait()
    loads[3].wait()
    l = [lab[a] == 1 for a in range(2)]

    @pl.loop(0, ROWS)
    def _(r):
        for h in range(2):
            for b in range(0, NYL, 32):
                u0, u1 = uv[0, r, h, b:b + 32], uv[1, r, h, b:b + 32]
                for a in range(2):
                    e = jnp.exp(-0.5 * jnp.where(l[a], u1, u0))
                    inv = 1.0 / e
                    c[a, r + 3, h, Y0 + b:Y0 + b + 32] = e / fv[a, r, h, b:b + 32]
                    c[2 + a, r + 3, h, Y0 + b:Y0 + b + 32] = (0.16 * e) * e
                    ifac[a, r, h, b:b + 32] = inv

    own = pl.ds(Y0, NYL)
    lo_in, lo_out = pl.ds(Y0, 8), pl.ds(Y0 - 8, 8)
    hi_in, hi_out = pl.ds(Y0 + NYL - 8, 8), pl.ds(Y0 + NYL, 8)
    UPS = (pl.ds(4, 3), pl.ds(0, 3))
    DNS = (pl.ds(3, 3), pl.ds(7, 3))
    OWN = (pl.ds(3, 4), pl.ds(3, 4))

    def halo(buf, first, ss, rs_):
        out = []
        k = first
        for dev, rows in ((around[2], OWN), (around[3], UPS), (around[4], DNS)):
            for a, b in ((lo_in, hi_out), (hi_in, lo_out)):
                out.append(send(buf(rows[0], a), buf(rows[1], b), ss.at[k], rs_.at[k], dev))
                k += 1
        return out

    coef = []
    coef.append(send(c.at[pl.ds(0, 2), UPS[0], :, own], c.at[pl.ds(0, 2), UPS[1], :, own], hsend.at[0], hrecv.at[0], around[0]))
    coef.append(send(c.at[pl.ds(0, 2), DNS[0], :, own], c.at[pl.ds(0, 2), DNS[1], :, own], hsend.at[1], hrecv.at[1], around[1]))
    coef.append(send(c.at[pl.ds(2, 2), pl.ds(5, 2), :, own], c.at[pl.ds(2, 2), pl.ds(1, 2), :, own], hsend.at[2], hrecv.at[2], around[0]))
    coef.append(send(c.at[pl.ds(2, 2), pl.ds(3, 2), :, own], c.at[pl.ds(2, 2), pl.ds(7, 2), :, own], hsend.at[3], hrecv.at[3], around[1]))
    coef += halo(lambda r_, y_: c.at[:, r_, :, y_], 4, hsend, hrecv)
    sent += coef

    for cp in rs:
        cp.wait_recv()
    for b in range(0, NYL, 32):
        acc = p[y, x, b:b + 32]
        for d in range(1, 8):
            acc = acc * prx[d, b:b + 32]
        pext[3 + y, x, Y0 + b:Y0 + b + 32] = acc
    ag = []
    mine = pext.at[3 + y, x, own]
    for d in range(1, 8):
        ag.append(send(mine, mine, psend.at[8 + d], precv.at[8 + d], arm_dev(d)))
    sent += ag
    for cp in ag:
        cp.wait_recv()

    ph = []
    ph.append(send(pext.at[UPS[0], :, own], pext.at[UPS[1], :, own], hsend.at[10], hrecv.at[10], around[0]))
    ph.append(send(pext.at[DNS[0], :, own], pext.at[DNS[1], :, own], hsend.at[11], hrecv.at[11], around[1]))
    ph += halo(lambda r_, y_: pext.at[r_, :, y_], 12, hsend, hrecv)
    sent += ph

    for cp in coef:
        cp.wait_recv()
    for cp in ph:
        cp.wait_recv()

    @pl.loop(0, 10)
    def _(r):
        for h in range(2):
            for b in range(8, 152, BLK):
                q = pext[r, h, b:b + BLK]
                for a in range(2):
                    va[a, r, h, b:b + BLK] = q * c[a, r, h, b:b + BLK]

    lane = lax.broadcasted_iota(jnp.int32, (BLK, LANES), 1)

    def advance(src, a, r, b, n, active):
        first, last = lane[:n] == 0, lane[:n] == LANES - 1
        v = [src[a, r, h, b:b + n] for h in range(2)]
        fwd_ = [pltpu.roll(t, 1, 1) for t in v]
        bwd = [pltpu.roll(t, LANES - 1, 1) for t in v]
        out = []
        for h in range(2):
            s = src[a, r - 1, h, b:b + n] + src[a, r + 1, h, b:b + n]
            s = s + (src[a, r, h, b - 1:b + n - 1] + src[a, r, h, b + 1:b + n + 1])
            s = s + (jnp.where(first, fwd_[1 - h], fwd_[h]) + jnp.where(last, bwd[1 - h], bwd[h]))
            new = c[2 + a, r, h, b:b + n] * (0.25 * v[h] + s)
            out.append(jnp.where(active, new, v[h]))
        return out

    for t, (src, dst) in enumerate(((va, vb), (vb, va))):
        for a in range(2):
            active = length[a] > t

            @pl.loop(1 + t, 9 - t)
            def _(r):
                for b in range(8, 152, BLK):
                    out = advance(src, a, r, b, BLK, active)
                    for h in range(2):
                        dst[a, r, h, b:b + BLK] = out[h]

    loads[4].wait()
    loads[5].wait()
    ds_ = []
    for i in range(1, 5):
        r = ys[i % 4]
        for b in range(0, NYL, 16):
            w = []
            for a in range(2):
                out = advance(va, a, r + 3, Y0 + b, 16, length[a] > 2)
                ws = []
                for h in range(2):
                    q = out[h] * ifac[a, r, h, b:b + 16]
                    cj[a, r, h, b:b + 16] = q
                    ws.append(q * pv[a, r, h, b:b + 16])
                w.append(ws)
            for h in range(2):
                one = jnp.where(l[0], w[0][h], 0.0) + jnp.where(l[1], w[1][h], 0.0)
                zero = jnp.where(l[0], 0.0, w[0][h]) + jnp.where(l[1], 0.0, w[1][h])
                dp[0, r, h, b:b + 16] = zero
                dp[1, r, h, b:b + 16] = one
        for j in (i % 4, i % 4 + 4):
            if j:
                px, py = peers[j]
                ds_.append(send(dp.at[px, py], drx.at[j], dsend.at[j], drecv.at[j], arm_dev(j)))
    sent += ds_
    stores = []
    for h in range(2):
        cp = pltpu.make_async_copy(cj.at[:, :, h], conj.at[:, :, :, pl.ds(h * LANES, LANES)], lsem.at[6 + h])
        cp.start()
        stores.append(cp)
    for cp in ds_:
        cp.wait_recv()
    for h in range(2):
        for b in range(0, NYL, 32):
            acc = dp[x, y, h, b:b + 32]
            for d in range(1, 8):
                acc = acc + drx[d, h, b:b + 32]
            do[x, y, h, b:b + 32] = acc
    dg = []
    piece = do.at[x, y]
    for d in range(1, 8):
        dg.append(send(piece, piece, dsend.at[8 + d], drecv.at[8 + d], arm_dev(d)))
    sent += dg
    for cp in dg:
        cp.wait_recv()
    for h in range(2):
        cp = pltpu.make_async_copy(do.at[:, :, h], dens.at[:, :, :, pl.ds(h * LANES, LANES)], lsem.at[8 + h])
        cp.start()
        stores.append(cp)
    for cp in sent:
        cp.wait_send()
    for cp in stores:
        cp.wait()


def local(forward_end, partner_end, potential, species_label, arm_length):
    full = (2, ROWS, 2, NYL, LANES)
    ext = (10, 2, YD, LANES)
    dma = pltpu.SemaphoreType.DMA
    return pl.pallas_call(
        kernel,
        name="star",
        out_shape=[jax.ShapeDtypeStruct(forward_end.shape, F32), jax.ShapeDtypeStruct(potential.shape, F32)],
        in_specs=[pl.BlockSpec(memory_space=pltpu.SMEM)] * 2 + [pl.BlockSpec(memory_space=pl.ANY)] * 3,
        out_specs=[pl.BlockSpec(memory_space=pl.ANY)] * 2,
        scratch_shapes=[
            pltpu.VMEM(full, F32), pltpu.VMEM(full, F32), pltpu.VMEM(full, F32),
            pltpu.VMEM((ROWS, 2, NYL, LANES), F32), pltpu.VMEM((8, NYL, LANES), F32),
            pltpu.VMEM(ext, F32), pltpu.VMEM((4,) + ext, F32), pltpu.VMEM(full, F32),
            pltpu.VMEM((2,) + ext, F32), pltpu.VMEM((2,) + ext, F32), pltpu.VMEM(full, F32),
            pltpu.VMEM(full, F32), pltpu.VMEM((8, 2, NYL, LANES), F32), pltpu.VMEM(full, F32),
            dma((10,)), dma((1,)), dma((1,)), dma((16,)), dma((16,)), dma((18,)), dma((18,)), dma((16,)), dma((16,)),
        ],
        compiler_params=pltpu.CompilerParams(collective_id=0, has_side_effects=True, vmem_limit_bytes=50 << 20),
        cost_estimate=pl.CostEstimate(flops=20_000_000, bytes_accessed=5 << 20, transcendentals=1 << 19),
    )(species_label, arm_length, forward_end, partner_end, potential)


def solution(mesh):
    return jax.shard_map(
        local,
        mesh=mesh,
        in_specs=(
            P("arm", "sx", "sy", None),
            P("arm", "sx", "sy", None),
            P(None, "sx", "sy", None),
            P("arm"),
            P("arm"),
        ),
        out_specs=(P("arm", "sx", "sy", None), P(None, "sx", "sy", None)),
        check_vma=False,
    )
```

time: 282 us -> 84.5 us (0.30)
  the two profiles are of different devices: /device:TPU:4 before, /device:TPU:2 now
where the time goes in v1:
time: 84.5 us; the launch traced here: 84.4 us
  Pallas kernels  79.3 us (94%)
  local copies, waits for them, and re-layouts  4.47 us (5%)
    pallas_call x1, Pallas kernels, local(): pl.pallas_call(kernel, name='star', out_shape=[jax.ShapeDtypeStruct(forwa...  79.3 us
    unnamed x8, local copies, waits for them, and re-layouts  4.47 us

profile of v1, /device:TPU:2, one launch (start us, length us, event | category | flops | bytes accessed | tf_op | source)
XLA Modules:
  0.0 84.4 jit_solution(16242989281099071043)
XLA Ops:
  0.6 0.0 copy-start
  0.6 1.2 %copy-done = f32[2,4,128,256]{3,2,1,0:T(8,128)S(1)} copy-done((f32[2,4,128,256]{3,2,1,0:T(8,128)S(1)}, f32[2,4,128,256]{3,2,1,0:T(8,128)}, u32[]{:S(2)}) %copy-start) | copy-done | bytes 1048600
  1.9 0.0 copy-start.1
  1.9 0.7 copy-done.1
  2.5 0.0 copy-start.2
  2.5 0.7 copy-done.2
  3.2 79.3 %star.1 = (f32[2,4,128,256]{3,2,1,0:T(8,128)S(1)}, f32[2,4,128,256]{3,2,1,0:T(8,128)S(1)}) custom-call(s32[2]{0:T(128)S(1)} %copy-done.1, s32[2]{0:T(128)S(1)} %copy-done.2, f32[2,4,128,256]{3,2,1,0:T(8,128)S(1)} %copy-done, f32[2,4,128,256]{3,2,1,0:T(8,128)} %par.1, f32[2,4,128,256]{3,2,1,0:T(8,128)} %pot.1), custom_call_target="tpu_custom_call" | custom-call | flops 20000000 | bytes 5242880 | tf_op jit(solution)/shard_map/star/pallas_call | solution.py:233
  82.4 1.0 %copy.9 = f32[2,4,128,256]{3,2,1,0:T(8,128)} copy(f32[2,4,128,256]{3,2,1,0:T(8,128)S(1)} %get-tuple-element.4) | data formatting | bytes 2097152
  83.4 1.0 %copy.10 = f32[2,4,128,256]{3,2,1,0:T(8,128)} copy(f32[2,4,128,256]{3,2,1,0:T(8,128)S(1)} %get-tuple-element.5) | data formatting | bytes 2097152
Async XLA Ops:
  0.6 1.2 %copy-start = (f32[2,4,128,256]{3,2,1,0:T(8,128)S(1)}, f32[2,4,128,256]{3,2,1,0:T(8,128)}, u32[]{:S(2)}) copy-start(f32[2,4,128,256]{3,2,1,0:T(8,128)} %fwd.1) | copy-start | bytes 3145732
  1.9 0.7 copy-start.1
  2.5 0.7 copy-start.2

commit v2 on v0

v2 whole, which is shorter than its diff:
```python
import jax
import jax.numpy as jnp
from jax import lax
from jax.experimental import pallas as pl
from jax.experimental.pallas import tpu as pltpu
from jax.sharding import PartitionSpec as P

MESH = pl.DeviceIdType.MESH
F32 = jnp.float32
ROWS, NYL, LANES = 4, 128, 128
YD, Y0 = 160, 16
SEG = (((0, 24, 80),), ((0, 104, 24), (24, 0, 24)))
YC = (80, 48)
DSEG = (((0, 32, 64),), ((0, 96, 32), (32, 0, 32)))
TILES = (tuple(range(3, 13)), (12, 13, 14, 15, 16, -1, 0, 1, 2, 3))
LAST = (tuple(range(4, 12)), (12, 13, 14, 15, 0, 1, 2, 3))


def kernel(
    lab_h, len_h, fwd, par, pot, conj, dens,
    lab, length, fv, pv, uv, p0, p1, prx0, prx1, pf0, pf1, g0, g1, q0, q1, ifac,
    es, ce, pes, pe, gp, v1, v2, v3, dp, drx,
    lsem, psend, precv, hsend, hrecv, dsend, drecv,
):
    arm, sx, sy = lax.axis_index("arm"), lax.axis_index("sx"), lax.axis_index("sy")
    x, y = arm // 4, arm % 4
    xs = [x, 1 - x]
    ys = [y, y + 1 - 2 * (y % 2), (y + 2) % 4, 3 - y]
    peers = [(xs[d // 4], ys[d % 4]) for d in range(8)]
    up, down, other = (sx + 1) % 32, (sx + 31) % 32, 1 - sy
    p, prx, pf, g, q = (p0, p1), (prx0, prx1), (pf0, pf1), (g0, g1), (q0, q1)

    def arm_dev(d):
        return {"arm": peers[d][0] * 4 + peers[d][1]}

    around = [{"sx": up}, {"sx": down}, {"sy": other}, {"sx": up, "sy": other}, {"sx": down, "sy": other}]

    loads = []
    for src, dst in ((fwd, fv), (pot, uv), (lab_h, lab), (len_h, length), (par, pv)):
        cp = pltpu.make_async_copy(src, dst, lsem.at[len(loads)])
        cp.start()
        loads.append(cp)
    stores = []
    sent = []

    def send(src, dst, ssem, rsem, k, dev):
        cp = pltpu.make_async_remote_copy(
            src_ref=src, dst_ref=dst, send_sem=ssem.at[k], recv_sem=rsem.at[k], device_id=dev, device_id_type=MESH
        )
        cp.start()
        sent.append(cp)
        return cp

    barrier = pltpu.get_barrier_semaphore()
    for d in range(1, 8):
        pl.semaphore_signal(barrier, inc=1, device_id=arm_dev(d), device_id_type=MESH)
    for dev in around:
        pl.semaphore_signal(barrier, inc=1, device_id=dev, device_id_type=MESH)

    loads[0].wait()

    def lanes(h):
        return slice(h * LANES, (h + 1) * LANES)

    @pl.loop(0, ROWS)
    def _(r):
        for k in range(2):
            for o, s, n in SEG[k]:
                for h in range(2):
                    p[k][r, h, o:o + n] = fv[0, r, s:s + n, lanes(h)] * fv[1, r, s:s + n, lanes(h)]

    pl.semaphore_wait(barrier, 12)


    rs = [[], []]
    for k in range(2):
        for d in range(1, 8):
            px, py = peers[d]
            rs[k].append(send(p[k].at[py, px], prx[k].at[d], psend, precv, 16 * k + d, arm_dev(d)))


    for i in (1, 2, 3):
        loads[i].wait()
    l = [lab[a] == 1 for a in range(2)]

    g_rows = ((pl.ds(4, 3), pl.ds(0, 3)), (pl.ds(3, 3), pl.ds(7, 3)))
    q_rows = ((pl.ds(5, 2), pl.ds(1, 2)), (pl.ds(3, 2), pl.ds(7, 2)))
    coef = [[], []]
    for k in range(2):

        @pl.loop(0, ROWS)
        def _(r):
            for o, s, n in SEG[k]:
                for h in range(2):
                    for b in range(0, n, 8):
                        ya, oa = s + b, o + b
                        u0, u1 = (uv[i, r, ya:ya + 8, lanes(h)] for i in range(2))
                        for a in range(2):
                            e = jnp.exp(-0.5 * jnp.where(l[a], u1, u0))
                            ge = e / fv[a, r, ya:ya + 8, lanes(h)]
                            qe = (0.16 * e) * e
                            g[k][r + 3, a, h, oa:oa + 8] = ge
                            q[k][r + 3, a, h, oa:oa + 8] = qe
                            ifac[a, r, ya:ya + 8, lanes(h)] = 1.0 / e
                            i, j = a * 6 + h * 3, 12 + a * 4 + h * 2
                            if ya == 0:
                                es[0, r, i:i + 3] = ge[0:3]
                                es[0, r, j:j + 2] = qe[0:2]
                            if ya == NYL - 8:
                                es[1, r, i:i + 3] = ge[5:8]
                                es[1, r, j:j + 2] = qe[6:8]

        for i in range(2):
            coef[k].append(send(g[k].at[g_rows[i][0]], g[k].at[g_rows[i][1]], hsend, hrecv, 4 * k + i, around[i]))
            coef[k].append(send(q[k].at[q_rows[i][0]], q[k].at[q_rows[i][1]], hsend, hrecv, 4 * k + 2 + i, around[i]))

    def edges(src, dst, first):
        out = []
        for dev, rows, to in ((2, pl.ds(0, 4), pl.ds(3, 4)), (3, pl.ds(1, 3), pl.ds(0, 3)), (4, pl.ds(0, 3), pl.ds(7, 3))):
            for side in range(2):
                out.append(send(src.at[side, rows], dst.at[side, to], hsend, hrecv, first + len(out), around[dev]))
        return out

    coef[1] += edges(es, ce, 8)


    ag = [[], []]
    for k in range(2):
        for cp in rs[k]:
            cp.wait_recv()
        for b in range(0, YC[k], 16):
            acc = p[k][y, x, b:b + 16]
            for d in range(1, 8):
                acc = acc * prx[k][d, b:b + 16]
            pf[k][3 + y, x, b:b + 16] = acc
        mine = pf[k].at[3 + y, x]
        for d in range(1, 8):
            ag[k].append(send(mine, mine, psend, precv, 16 * k + 8 + d, arm_dev(d)))


    ph = [[], []]
    for k in range(2):
        for cp in ag[k]:
            cp.wait_recv()
        for i in range(2):
            ph[k].append(send(pf[k].at[g_rows[i][0]], pf[k].at[g_rows[i][1]], hsend, hrecv, 14 + 2 * k + i, around[i]))
        if k == 1:
            for r in range(ROWS):
                for h in range(2):
                    pes[0, r, 3 * h:3 * h + 3] = pf1[r + 3, h, 24:27]
                    pes[1, r, 3 * h:3 * h + 3] = pf1[r + 3, h, 21:24]
            ph[1] += edges(pes, pe, 18)


    lane = lax.broadcasted_iota(jnp.int32, (8, LANES), 1)
    first, last = lane == 0, lane == LANES - 1

    def q_tile(a, r, h, t):
        if t in (-1, 16):
            return gp[0 if t == 16 else 1, r, a, h]
        if 3 <= t < 13:
            return q0[r, a, h, 8 * t - 24:8 * t - 16]
        o = 8 * t - 104 if t >= 13 else 8 * t + 24
        return q1[r, a, h, o:o + 8]

    def advance(src, a, r, t, active):
        b = Y0 + 8 * t
        v = [src[a, r, h, b:b + 8] for h in range(2)]
        right = [pltpu.roll(w, 1, 1) for w in v]
        left = [pltpu.roll(w, LANES - 1, 1) for w in v]
        out = []
        for h in range(2):
            s = src[a, r - 1, h, b:b + 8] + src[a, r + 1, h, b:b + 8]
            s = s + (src[a, r, h, b - 1:b + 7] + src[a, r, h, b + 1:b + 9])
            s = s + (jnp.where(first, right[1 - h], right[h]) + jnp.where(last, left[1 - h], left[h]))
            new = q_tile(a, r, h, t) * (0.25 * v[h] + s)
            out.append(jnp.where(active, new, v[h]))
        return out

    loads[4].wait()
    drs = [[], []]
    for k in range(2):
        for cp in coef[k]:
            cp.wait_recv()
        for cp in ph[k]:
            cp.wait_recv()

        @pl.loop(0, 10)
        def _(r):
            for o, s, n in SEG[k]:
                for h in range(2):
                    f = pf[k][r, h, o:o + n]
                    for a in range(2):
                        v1[a, r, h, Y0 + s:Y0 + s + n] = f * g[k][r, a, h, o:o + n]
            if k == 1:
                for side, b in ((0, Y0 + NYL), (1, Y0 - 3)):
                    for h in range(2):
                        f = pe[side, r, 3 * h:3 * h + 3]
                        for a in range(2):
                            i, j = a * 6 + h * 3, 12 + a * 4 + h * 2
                            v1[a, r, h, b:b + 3] = f * ce[side, r, i:i + 3]
                            gp[side, r, a, h, 6 * side:6 * side + 2] = ce[side, r, j:j + 2]

        for t, (src, dst) in enumerate(((v1, v2), (v2, v3))):
            act = [length[a] > t for a in range(2)]

            @pl.loop(1 + t, 9 - t)
            def _(r):
                for tile in TILES[k]:
                    b = Y0 + 8 * tile
                    for a in range(2):
                        out = advance(src, a, r, tile, act[a])
                        for h in range(2):
                            dst[a, r, h, b:b + 8] = out[h]

        act = [length[a] > 2 for a in range(2)]
        for i in (1, 2, 3, 0):
            r = ys[i]
            for n, tile in enumerate(LAST[k]):
                b = 8 * tile
                w = []
                for a in range(2):
                    out = advance(v3, a, r + 3, tile, act[a])
                    ws = []
                    for h in range(2):
                        c = out[h] * ifac[a, r, b:b + 8, lanes(h)]
                        conj[a, r, b:b + 8, lanes(h)] = c
                        ws.append(c * pv[a, r, b:b + 8, lanes(h)])
                    w.append(ws)
                for h in range(2):
                    dp[k, 0, r, 8 * n:8 * n + 8, lanes(h)] = jnp.where(l[0], 0.0, w[0][h]) + jnp.where(l[1], 0.0, w[1][h])
                    dp[k, 1, r, 8 * n:8 * n + 8, lanes(h)] = jnp.where(l[0], w[0][h], 0.0) + jnp.where(l[1], w[1][h], 0.0)
            for j in (i, i + 4):
                if j:
                    px, py = peers[j]
                    drs[k].append(send(dp.at[k, px, py], drx.at[k, j], dsend, drecv, 24 * k + j, arm_dev(j)))


    dag = []
    for k in range(2):
        for cp in drs[k]:
            cp.wait_recv()
        for m, (o, s, n) in enumerate(DSEG[k]):
            for h in range(2):
                for b in range(0, n, 16):
                    acc = dp[k, x, y, o + b:o + b + 16, lanes(h)]
                    for d in range(1, 8):
                        acc = acc + drx[k, d, o + b:o + b + 16, lanes(h)]
                    dens[x, y, s + b:s + b + 16, lanes(h)] = acc
            piece = dens.at[x, y, pl.ds(s, n)]
            for d in range(1, 8):
                dag.append(send(piece, piece, dsend, drecv, 24 * k + 8 * (m + 1) + d, arm_dev(d)))

    for cp in dag:
        cp.wait_recv()
    for cp in sent:
        cp.wait_send()


def local(forward_end, partner_end, potential, species_label, arm_length):
    full = pltpu.VMEM((2, ROWS, NYL, 2 * LANES), F32)
    dma = pltpu.SemaphoreType.DMA

    def v(*shape):
        return pltpu.VMEM(shape, F32)

    return pl.pallas_call(
        kernel,
        name="star",
        out_shape=[jax.ShapeDtypeStruct(forward_end.shape, F32), jax.ShapeDtypeStruct(potential.shape, F32)],
        in_specs=[pl.BlockSpec(memory_space=pltpu.HBM)] * 5,
        out_specs=[pl.BlockSpec(memory_space=pltpu.VMEM)] * 2,
        scratch_shapes=[
            pltpu.SMEM((2,), jnp.int32), pltpu.SMEM((2,), jnp.int32), full, full, full,
            v(ROWS, 2, YC[0], LANES), v(ROWS, 2, YC[1], LANES),
            v(8, YC[0], LANES), v(8, YC[1], LANES),
            v(10, 2, YC[0], LANES), v(10, 2, YC[1], LANES),
            v(10, 2, 2, YC[0], LANES), v(10, 2, 2, YC[1], LANES),
            v(10, 2, 2, YC[0], LANES), v(10, 2, 2, YC[1], LANES),
            full,
            v(2, ROWS, 24, LANES), v(2, 10, 24, LANES), v(2, ROWS, 8, LANES), v(2, 10, 8, LANES),
            v(2, 10, 2, 2, 8, LANES),
            v(2, 10, 2, YD, LANES), v(2, 10, 2, YD, LANES), v(2, 10, 2, YD, LANES),
            v(2, 2, ROWS, 64, 2 * LANES), v(2, 8, 64, 2 * LANES),
            dma((5,)), dma((32,)), dma((32,)), dma((24,)), dma((24,)), dma((48,)), dma((48,)),
        ],
        compiler_params=pltpu.CompilerParams(collective_id=0, has_side_effects=True, vmem_limit_bytes=51 << 20),
        cost_estimate=pl.CostEstimate(flops=20_000_000, bytes_accessed=5 << 20, transcendentals=1 << 19),
    )(species_label, arm_length, forward_end, partner_end, potential)


def solution(mesh):
    return jax.shard_map(
        local,
        mesh=mesh,
        in_specs=(
            P("arm", "sx", "sy", None),
            P("arm", "sx", "sy", None),
            P(None, "sx", "sy", None),
            P("arm"),
            P("arm"),
        ),
        out_specs=(P("arm", "sx", "sy", None), P(None, "sx", "sy", None)),
        check_vma=False,
    )
```

time: 282 us -> 63.1 us (0.22)
  the two profiles are of different devices: /device:TPU:4 before, /device:TPU:2 now
where the time goes in v2:
time: 63.1 us; the launch traced here: 62.9 us
  Pallas kernels  59 us (94%)
  local copies, waits for them, and re-layouts  3.25 us (5%)
  between operations  0.65 us (1%)
    pallas_call x1, Pallas kernels, local(): pl.pallas_call(kernel, name='star', out_shape=[jax.ShapeDtypeStruct(forwa...  59 us
    unnamed x6, local copies, waits for them, and re-layouts  3.25 us

profile of v2, /device:TPU:2, one launch (start us, length us, event | category | flops | bytes accessed | tf_op | source)
XLA Modules:
  0.0 62.9 jit_solution(17249502414027142624)
XLA Ops:
  0.6 0.0 copy-start
  0.6 0.6 %copy-done = s32[2]{0:T(128)S(1)} copy-done((s32[2]{0:T(128)S(1)}, s32[2]{0:T(128)}, u32[]{:S(2)}) %copy-start) | copy-done | bytes 32
  1.3 0.0 copy-start.1
  1.3 0.7 %copy-done.1 = s32[2]{0:T(128)S(1)} copy-done((s32[2]{0:T(128)S(1)}, s32[2]{0:T(128)}, u32[]{:S(2)}) %copy-start.1) | copy-done | bytes 32
  1.9 59.0 %star.1 = (f32[2,4,128,256]{3,2,1,0:T(8,128)S(1)}, f32[2,4,128,256]{3,2,1,0:T(8,128)S(1)}) custom-call(s32[2]{0:T(128)S(1)} %copy-done, s32[2]{0:T(128)S(1)} %copy-done.1, f32[2,4,128,256]{3,2,1,0:T(8,128)} %fwd.1, f32[2,4,128,256]{3,2,1,0:T(8,128)} %par.1, f32[2,4,128,256]{3,2,1,0:T(8,128)} %pot.1), custom_call_target="tpu_custom_call" | custom-call | flops 20000000 | bytes 5242880 | tf_op jit(solution)/shard_map/star/pallas_call | solution.py:267
  61.0 1.0 %copy.9 = f32[2,4,128,256]{3,2,1,0:T(8,128)} copy(f32[2,4,128,256]{3,2,1,0:T(8,128)S(1)} %get-tuple-element.4) | data formatting | bytes 2097152
  61.9 1.0 %copy.10 = f32[2,4,128,256]{3,2,1,0:T(8,128)} copy(f32[2,4,128,256]{3,2,1,0:T(8,128)S(1)} %get-tuple-element.5) | data formatting | bytes 2097152
Async XLA Ops:
  0.6 0.7 %copy-start = (s32[2]{0:T(128)S(1)}, s32[2]{0:T(128)}, u32[]{:S(2)}) copy-start(s32[2]{0:T(128)} %lab_h.1) | copy-start | bytes 28
  1.3 0.7 %copy-start.1 = (s32[2]{0:T(128)S(1)}, s32[2]{0:T(128)}, u32[]{:S(2)}) copy-start(s32[2]{0:T(128)} %len_h.1) | copy-start | bytes 28

commit v3 on v2

v3 whole, which is shorter than its diff:
```python
import jax
import jax.numpy as jnp
from jax import lax
from jax.experimental import pallas as pl
from jax.experimental.pallas import tpu as pltpu
from jax.sharding import PartitionSpec as P

MESH = pl.DeviceIdType.MESH
F32 = jnp.float32
ROWS, NYL, LANES = 4, 128, 128
YD, Y0 = 160, 16
BOUNDS = ((40, 88), (8, 120), (0, 128))
RESULT = ((48, 80), (16, 112), (0, 128))
NC = len(BOUNDS)
DIRECT_P = (True, False, True)


def segments(bounds, k):
    lo, hi = bounds[k]
    if k == 0:
        return ((0, lo, hi - lo),)
    lo_in, hi_in = bounds[k - 1]
    return ((0, hi_in, hi - hi_in), (hi - hi_in, lo, lo_in - lo))


SEG = [segments(BOUNDS, k) for k in range(NC)]
YC = [sum(n for _, _, n in s) for s in SEG]
HALF = [((48, 16), (64, 16))] + [tuple((s, n) for _, s, n in segments(RESULT, k)) for k in range(1, NC)]
TILES = [tuple(range(BOUNDS[0][0] // 8, BOUNDS[0][1] // 8))]
for _k in range(1, NC):
    _end = 1 if _k == NC - 1 else 0
    TILES.append(
        tuple(range(BOUNDS[_k - 1][1] // 8 - 1, BOUNDS[_k][1] // 8 + _end))
        + tuple(range(BOUNDS[_k][0] // 8 - _end, BOUNDS[_k - 1][0] // 8 + 1))
    )
SEMS = 7 * NC + 3 - sum(DIRECT_P)
PLACE = {}
for _k in range(NC):
    for _o, _s, _n in SEG[_k]:
        for _b in range(0, _n, 8):
            PLACE[(_s + _b) // 8] = (_k, _o + _b)


def lanes(h):
    return slice(h * LANES, (h + 1) * LANES)


def kernel(lab_h, len_h, fwd, par, pot, conj, dens, *scratch):
    scratch = list(scratch)

    def take(n):
        out = scratch[:n]
        del scratch[:n]
        return out

    lab, length, fv, pv, uv, ifac, es, ce, pes, pe, gp, v1, v2, v3 = take(14)
    p, prx, pxx, pf, g, q = (take(NC) for _ in range(6))
    da, rxa = (take(NC) for _ in range(2))
    lsem, ssem, rsem = take(3)

    arm, sx, sy = lax.axis_index("arm"), lax.axis_index("sx"), lax.axis_index("sy")
    x, y = arm // 4, arm % 4
    ox = 1 - x
    ys = [y, y + 1 - 2 * (y % 2), (y + 2) % 4, 3 - y]
    peers = [((x, ox)[d // 4], ys[d % 4]) for d in range(8)]
    up, down, other = (sx + 1) % 32, (sx + 31) % 32, 1 - sy

    def arm_dev(d):
        return {"arm": peers[d][0] * 4 + peers[d][1]}

    around = [{"sx": up}, {"sx": down}, {"sy": other}, {"sx": up, "sy": other}, {"sx": down, "sy": other}]

    quarters = [pl.ds(r, 1) for r in range(ROWS)]
    for r in quarters:
        pltpu.make_async_copy(fwd.at[:, r], fv.at[:, r], lsem.at[0]).start()
    for i, (src, dst) in enumerate(((pot, uv), (lab_h, lab), (len_h, length), (par, pv))):
        pltpu.make_async_copy(src, dst, lsem.at[i + 1]).start()

    def loaded(i, src, dst):
        pltpu.make_async_copy(src, dst, lsem.at[i]).wait()

    groups = {}

    def send(group, src, dst, dev):
        n = groups.setdefault(group, len(groups))
        pltpu.make_async_remote_copy(
            src_ref=src, dst_ref=dst, send_sem=ssem.at[n], recv_sem=rsem.at[n], device_id=dev, device_id_type=MESH
        ).start()

    sizes = []

    def arrived(group, like):
        pltpu.make_async_copy(like, like, rsem.at[groups[group]]).wait()
        sizes.append((group, like))

    barrier = pltpu.get_barrier_semaphore()
    for d in range(1, 8):
        pl.semaphore_signal(barrier, inc=1, device_id=arm_dev(d), device_id_type=MESH)
    for dev in around:
        pl.semaphore_signal(barrier, inc=1, device_id=dev, device_id_type=MESH)

    loaded(0, fwd, fv)

    @pl.loop(0, ROWS)
    def _(r):
        for k in range(NC):
            for o, s, n in SEG[k]:
                for h in range(2):
                    p[k][r, h, o:o + n] = fv[0, r, s:s + n, lanes(h)] * fv[1, r, s:s + n, lanes(h)]

    def work_out(k):
        @pl.loop(0, ROWS)
        def _(r):
            for o, s, n in SEG[k]:
                for h in range(2):
                    for b in range(0, n, 8):
                        ya, oa = s + b, o + b
                        u0, u1 = (uv[i, r, ya:ya + 8, lanes(h)] for i in range(2))
                        for a in range(2):
                            e = jnp.exp(-0.5 * jnp.where(l[a], u1, u0))
                            ge = e / fv[a, r, ya:ya + 8, lanes(h)]
                            qe = (0.16 * e) * e
                            g[k][r + 3, a, h, oa:oa + 8] = ge
                            q[k][r + 3, a, h, oa:oa + 8] = qe
                            ifac[a, r, ya:ya + 8, lanes(h)] = 1.0 / e
                            i, j = a * 6 + h * 3, 12 + a * 4 + h * 2
                            if ya == 0:
                                es[0, r, i:i + 3] = ge[0:3]
                                es[0, r, j:j + 2] = qe[0:2]
                            if ya == NYL - 8:
                                es[1, r, i:i + 3] = ge[5:8]
                                es[1, r, j:j + 2] = qe[6:8]

    pl.semaphore_wait(barrier, 12)

    g_rows = ((pl.ds(4, 3), pl.ds(0, 3)), (pl.ds(3, 3), pl.ds(7, 3)))
    q_rows = ((pl.ds(5, 2), pl.ds(1, 2)), (pl.ds(3, 2), pl.ds(7, 2)))

    def edges(group, src, dst, corners):
        for side in range(2):
            send(group, src.at[side], dst.at[side, pl.ds(3, 4)], around[2])
            if corners:
                send(group, src.at[side, pl.ds(1, 3)], dst.at[side, pl.ds(0, 3)], around[3])
                send(group, src.at[side, pl.ds(0, 3)], dst.at[side, pl.ds(7, 3)], around[4])

    def forward_corners():
        arrived("edge", es)
        for side in range(2):
            send("corner", ce.at[side, pl.ds(4, 3)], ce.at[side, pl.ds(0, 3)], around[0])
            send("corner", ce.at[side, pl.ds(3, 3)], ce.at[side, pl.ds(7, 3)], around[1])

    def scatter(k):
        if DIRECT_P[k]:
            for d in range(1, 8):
                px, py = peers[d]
                send(f"rs{k}", p[k].at[py, px], prx[k].at[d], arm_dev(d))
        else:
            for d in (1, 2, 3):
                send(f"rs{k}", p[k].at[ys[d]], prx[k].at[pl.ds(2 * d, 2)], arm_dev(d))

    def coefficients(k):
        for i in range(2):
            send(f"coef{k}", g[k].at[g_rows[i][0]], g[k].at[g_rows[i][1]], around[i])
            send(f"coef{k}", q[k].at[q_rows[i][0]], q[k].at[q_rows[i][1]], around[i])

    def cross(k):
        if DIRECT_P[k]:
            return
        arrived(f"rs{k}", prx[k].at[pl.ds(2, 6)])
        for h in range(2):
            for b in range(0, YC[k], 16):
                c = slice(b, b + 16)
                prx[k][h, c] = (p[k][y, h, c] * prx[k][2 + h, c]) * (prx[k][4 + h, c] * prx[k][6 + h, c])
        send(f"xp{k}", prx[k].at[pl.ds(0, 2)], pxx[k], arm_dev(4))

    def gather(k):
        if DIRECT_P[k]:
            arrived(f"rs{k}", prx[k].at[pl.ds(1, 7)])
            for b in range(0, YC[k], 16):
                acc = p[k][y, x, b:b + 16]
                for d in range(1, 8):
                    acc = acc * prx[k][d, b:b + 16]
                pf[k][3 + y, x, b:b + 16] = acc
            mine = pf[k].at[3 + y, x]
            for d in range(1, 8):
                send(f"ag{k}", mine, mine, arm_dev(d))
        else:
            arrived(f"xp{k}", pxx[k])
            for h in range(2):
                for b in range(0, YC[k], 16):
                    pf[k][3 + y, h, b:b + 16] = prx[k][h, b:b + 16] * pxx[k][h, b:b + 16]
            mine = pf[k].at[3 + y]
            for d in (1, 2, 3):
                send(f"ag{k}", mine, mine, arm_dev(d))

    def product_halo(k):
        arrived(f"ag{k}", prx[k].at[pl.ds(1, 7) if DIRECT_P[k] else pl.ds(2, 6)])
        for i in range(2):
            send(f"ph{k}", pf[k].at[g_rows[i][0]], pf[k].at[g_rows[i][1]], around[i])
        if k == NC - 1:
            k0, o0 = PLACE[0]
            k1, o1 = PLACE[NYL // 8 - 1]
            for r in range(ROWS):
                for h in range(2):
                    pes[0, r, 3 * h:3 * h + 3] = pf[k0][r + 3, h, o0:o0 + 3]
                    pes[1, r, 3 * h:3 * h + 3] = pf[k1][r + 3, h, o1 + 5:o1 + 8]
            edges("pe", pes, pe, True)

    scatter(0)
    scatter(2)
    loaded(1, pot, uv)
    loaded(2, lab_h, lab)
    loaded(3, len_h, length)
    l = [lab[a] == 1 for a in range(2)]
    work_out(0)
    coefficients(0)
    work_out(2)
    scatter(1)
    coefficients(2)
    edges("edge", es, ce, False)
    work_out(1)
    gather(0)
    gather(2)
    coefficients(1)
    cross(1)
    forward_corners()
    gather(1)
    product_halo(0)
    product_halo(2)
    product_halo(1)

    lane = lax.broadcasted_iota(jnp.int32, (8, LANES), 1)
    first, last = lane == 0, lane == LANES - 1

    def q_tile(a, r, h, t):
        if t in (-1, 16):
            return gp[0 if t == 16 else 1, r, a, h]
        k, o = PLACE[t]
        return q[k][r, a, h, o:o + 8]

    def advance(src, a, r, t, active):
        b = Y0 + 8 * t
        v = [src[a, r, h, b:b + 8] for h in range(2)]
        right = [pltpu.roll(w, 1, 1) for w in v]
        left = [pltpu.roll(w, LANES - 1, 1) for w in v]
        out = []
        for h in range(2):
            s = src[a, r - 1, h, b:b + 8] + src[a, r + 1, h, b:b + 8]
            s = s + (src[a, r, h, b - 1:b + 7] + src[a, r, h, b + 1:b + 9])
            s = s + (jnp.where(first, right[1 - h], right[h]) + jnp.where(last, left[1 - h], left[h]))
            new = q_tile(a, r, h, t) * (0.25 * v[h] + s)
            out.append(jnp.where(active, new, v[h]))
        return out

    def steps(k):
        arrived(f"coef{k}", g[k])
        arrived(f"ph{k}", pf[k].at[pl.ds(0, 6)])
        if k == NC - 1:
            arrived("corner", ce.at[:, pl.ds(0, 6)])
            arrived("pe", pe)

        @pl.loop(0, 10)
        def _(r):
            for o, s, n in SEG[k]:
                for h in range(2):
                    f = pf[k][r, h, o:o + n]
                    for a in range(2):
                        v1[a, r, h, Y0 + s:Y0 + s + n] = f * g[k][r, a, h, o:o + n]
            if k == NC - 1:
                for side, b in ((0, Y0 + NYL), (1, Y0 - 3)):
                    for h in range(2):
                        f = pe[side, r, 3 * h:3 * h + 3]
                        for a in range(2):
                            i, j = a * 6 + h * 3, 12 + a * 4 + h * 2
                            v1[a, r, h, b:b + 3] = f * ce[side, r, i:i + 3]
                            gp[side, r, a, h, 6 * side:6 * side + 2] = ce[side, r, j:j + 2]

        for t, (src, dst) in enumerate(((v1, v2), (v2, v3))):
            act = [length[a] > t for a in range(2)]

            @pl.loop(1 + t, 9 - t)
            def _(r):
                for tile in TILES[k]:
                    b = Y0 + 8 * tile
                    for a in range(2):
                        out = advance(src, a, r, tile, act[a])
                        for h in range(2):
                            dst[a, r, h, b:b + 8] = out[h]

        act = [length[a] > 2 for a in range(2)]
        for i in (1, 2, 3, 0):
            r = ys[i]
            for half in range(2):
                s0, n0 = HALF[k][half]
                for m in range(0, n0, 8):
                    b = s0 + m
                    w = []
                    for a in range(2):
                        out = advance(v3, a, r + 3, b // 8, act[a])
                        ws = []
                        for h in range(2):
                            c = out[h] * ifac[a, r, b:b + 8, lanes(h)]
                            conj[a, r, b:b + 8, lanes(h)] = c
                            ws.append(c * pv[a, r, b:b + 8, lanes(h)])
                        w.append(ws)
                    for h in range(2):
                        zero = jnp.where(l[0], 0.0, w[0][h]) + jnp.where(l[1], 0.0, w[1][h])
                        one = jnp.where(l[0], w[0][h], 0.0) + jnp.where(l[1], w[1][h], 0.0)
                        o = m + half * n0
                        da[k][0, r, o:o + 8, lanes(h)] = zero
                        da[k][1, r, o:o + 8, lanes(h)] = one
            for j in (i, i + 4):
                if j:
                    px, py = peers[j]
                    send(f"drs{k}", da[k].at[px, py], rxa[k].at[j], arm_dev(j))

    def gather_density(k):
        arrived(f"drs{k}", rxa[k].at[pl.ds(1, 7)])
        o = 0
        for half, (s, n) in enumerate(HALF[k]):
            for h in range(2):
                for b in range(0, n, 8):
                    c = slice(o + b, o + b + 8)
                    acc = da[k][x, y, c, lanes(h)]
                    for d in range(1, 8):
                        acc = acc + rxa[k][d, c, lanes(h)]
                    dens[x, y, s + b:s + b + 8, lanes(h)] = acc
            o += n
            if k == 0 and half == 0:
                continue
            piece = dens.at[x, y, pl.ds(HALF[0][0][0], 2 * n) if k == 0 else pl.ds(s, n)]
            for d in range(1, 8):
                send(f"dag{k}", piece, piece, arm_dev(d))

    loaded(4, par, pv)
    for k in range(NC):
        steps(k)
    for k in range(NC):
        gather_density(k)
    for k in range(NC):
        arrived(f"dag{k}", rxa[k].at[pl.ds(1, 7)])
    for group, like in sizes:
        pltpu.make_async_copy(like, like, ssem.at[groups[group]]).wait()


def local(forward_end, partner_end, potential, species_label, arm_length):
    full = pltpu.VMEM((2, ROWS, NYL, 2 * LANES), F32)
    dma = pltpu.SemaphoreType.DMA

    def v(*shape):
        return pltpu.VMEM(shape, F32)

    wide = 2 * LANES
    nh = [h[0][1] for h in HALF]
    return pl.pallas_call(
        kernel,
        name="star",
        out_shape=[jax.ShapeDtypeStruct(forward_end.shape, F32), jax.ShapeDtypeStruct(potential.shape, F32)],
        in_specs=[pl.BlockSpec(memory_space=pl.ANY)] * 5,
        out_specs=[pl.BlockSpec(memory_space=pltpu.VMEM)] * 2,
        scratch_shapes=[
            pltpu.SMEM((2,), jnp.int32), pltpu.SMEM((2,), jnp.int32), full, full, full, full,
            v(2, ROWS, 24, LANES), v(2, 10, 24, LANES), v(2, ROWS, 8, LANES), v(2, 10, 8, LANES),
            v(2, 10, 2, 2, 8, LANES),
            v(2, 10, 2, YD, LANES), v(2, 10, 2, YD, LANES), v(2, 10, 2, YD, LANES),
        ]
        + [v(ROWS, 2, n, LANES) for n in YC]
        + [v(8, n, LANES) for n in YC]
        + [v(2, n, LANES) for n in YC]
        + [v(10, 2, n, LANES) for n in YC]
        + [v(10, 2, 2, n, LANES) for n in YC]
        + [v(10, 2, 2, n, LANES) for n in YC]
        + [v(2, ROWS, 2 * n, wide) for n in nh]
        + [v(8, 2 * n, wide) for n in nh]
        + [dma((n,)) for n in (5, SEMS, SEMS)],
        compiler_params=pltpu.CompilerParams(collective_id=0, has_side_effects=True, vmem_limit_bytes=51 << 20),
        cost_estimate=pl.CostEstimate(flops=20_000_000, bytes_accessed=5 << 20, transcendentals=1 << 19),
    )(species_label, arm_length, forward_end, partner_end, potential)


def solution(mesh):
    return jax.shard_map(
        local,
        mesh=mesh,
        in_specs=(
            P("arm", "sx", "sy", None),
            P("arm", "sx", "sy", None),
            P(None, "sx", "sy", None),
            P("arm"),
            P("arm"),
        ),
        out_specs=(P("arm", "sx", "sy", None), P(None, "sx", "sy", None)),
        check_vma=False,
    )
```

time: 63.1 us -> 60.9 us (0.965)
  Pallas kernels: 59 us -> 56.9 us
    pallas_call x1, Pallas kernels: 59 us -> 56.9 us  [local(): pl.pallas_call(kernel, name='star', out_shape=[jax.ShapeDtypeStruct(forwa...]
where the time goes in v3:
time: 60.9 us; the launch traced here: 60.8 us
  Pallas kernels  56.9 us (93%)
  local copies, waits for them, and re-layouts  3.25 us (5%)
  between operations  0.65 us (1%)
    pallas_call x1, Pallas kernels, local(): pl.pallas_call(kernel, name='star', out_shape=[jax.ShapeDtypeStruct(forwa...  56.9 us
    unnamed x6, local copies, waits for them, and re-layouts  3.25 us

profile of v3, /device:TPU:2, one launch (start us, length us, event | category | flops | bytes accessed | tf_op | source)
XLA Modules:
  0.0 60.8 jit_solution(609815784013212912)
XLA Ops:
  0.6 0.0 copy-start
  0.6 0.6 %copy-done = s32[2]{0:T(128)S(1)} copy-done((s32[2]{0:T(128)S(1)}, s32[2]{0:T(128)}, u32[]{:S(2)}) %copy-start) | copy-done | bytes 32
  1.3 0.0 copy-start.1
  1.3 0.7 %copy-done.1 = s32[2]{0:T(128)S(1)} copy-done((s32[2]{0:T(128)S(1)}, s32[2]{0:T(128)}, u32[]{:S(2)}) %copy-start.1) | copy-done | bytes 32
  1.9 56.9 %star.1 = (f32[2,4,128,256]{3,2,1,0:T(8,128)S(1)}, f32[2,4,128,256]{3,2,1,0:T(8,128)S(1)}) custom-call(s32[2]{0:T(128)S(1)} %copy-done, s32[2]{0:T(128)S(1)} %copy-done.1, f32[2,4,128,256]{3,2,1,0:T(8,128)} %fwd.1, f32[2,4,128,256]{3,2,1,0:T(8,128)} %par.1, f32[2,4,128,256]{3,2,1,0:T(8,128)} %pot.1), custom_call_target="tpu_custom_call" | custom-call | flops 20000000 | bytes 5242880 | tf_op jit(solution)/shard_map/star/pallas_call | solution.py:355
  58.8 1.0 %copy.9 = f32[2,4,128,256]{3,2,1,0:T(8,128)} copy(f32[2,4,128,256]{3,2,1,0:T(8,128)S(1)} %get-tuple-element.4) | data formatting | bytes 2097152
  59.8 1.0 %copy.10 = f32[2,4,128,256]{3,2,1,0:T(8,128)} copy(f32[2,4,128,256]{3,2,1,0:T(8,128)S(1)} %get-tuple-element.5) | data formatting | bytes 2097152
Async XLA Ops:
  0.6 0.7 %copy-start = (s32[2]{0:T(128)S(1)}, s32[2]{0:T(128)}, u32[]{:S(2)}) copy-start(s32[2]{0:T(128)} %lab_h.1) | copy-start | bytes 28
  1.3 0.7 %copy-start.1 = (s32[2]{0:T(128)S(1)}, s32[2]{0:T(128)}, u32[]{:S(2)}) copy-start(s32[2]{0:T(128)} %len_h.1) | copy-start | bytes 28

commit v4 on v3

--- a/solution.py
+++ b/solution.py
@@ -9,9 +9,10 @@
 F32 = jnp.float32
 ROWS, NYL, LANES = 4, 128, 128
 YD, Y0 = 160, 16
-BOUNDS = ((40, 88), (8, 120), (0, 128))
-RESULT = ((48, 80), (16, 112), (0, 128))
+BOUNDS = ((32, 96), (8, 120), (0, 128))
+RESULT = ((40, 88), (16, 112), (0, 128))
 NC = len(BOUNDS)
+TWO_LEVEL = (True, True, False)
 DIRECT_P = (True, False, True)
 
 
@@ -25,7 +26,8 @@
 
 SEG = [segments(BOUNDS, k) for k in range(NC)]
 YC = [sum(n for _, _, n in s) for s in SEG]
-HALF = [((48, 16), (64, 16))] + [tuple((s, n) for _, s, n in segments(RESULT, k)) for k in range(1, NC)]
+_lo, _n = RESULT[0][0], (RESULT[0][1] - RESULT[0][0]) // 2
+HALF = [((_lo, _n), (_lo + _n, _n))] + [tuple((s, n) for _, s, n in segments(RESULT, k)) for k in range(1, NC)]
 TILES = [tuple(range(BOUNDS[0][0] // 8, BOUNDS[0][1] // 8))]
 for _k in range(1, NC):
     _end = 1 if _k == NC - 1 else 0
@@ -33,7 +35,7 @@
         tuple(range(BOUNDS[_k - 1][1] // 8 - 1, BOUNDS[_k][1] // 8 + _end))
         + tuple(range(BOUNDS[_k][0] // 8 - _end, BOUNDS[_k - 1][0] // 8 + 1))
     )
-SEMS = 7 * NC + 3 - sum(DIRECT_P)
+SEMS = 7 * NC + 3 - sum(DIRECT_P) + sum(TWO_LEVEL)
 PLACE = {}
 for _k in range(NC):
     for _o, _s, _n in SEG[_k]:
@@ -317,7 +319,7 @@
     def gather_density(k):
         arrived(f"drs{k}", rxa[k].at[pl.ds(1, 7)])
         o = 0
-        for half, (s, n) in enumerate(HALF[k]):
+        for s, n in HALF[k]:
             for h in range(2):
                 for b in range(0, n, 8):
                     c = slice(o + b, o + b + 8)
@@ -326,10 +328,28 @@
                         acc = acc + rxa[k][d, c, lanes(h)]
                     dens[x, y, s + b:s + b + 8, lanes(h)] = acc
             o += n
-            if k == 0 and half == 0:
-                continue
-            piece = dens.at[x, y, pl.ds(HALF[0][0][0], 2 * n) if k == 0 else pl.ds(s, n)]
-            for d in range(1, 8):
+        parts = [dens.at[x, y, pl.ds(s, n)] for s, n in HALF[k]]
+        if TWO_LEVEL[k]:
+            send(f"first{k}", parts[1], parts[1], arm_dev(4))
+            for d in (1, 2, 3):
+                send(f"first{k}", parts[0], parts[0], arm_dev(d))
+            send(f"dag{k}", parts[0], parts[0], arm_dev(4))
+            for d in (1, 2, 3):
+                send(f"dag{k}", parts[1], parts[1], arm_dev(d))
+        else:
+            for piece in parts:
+                for d in range(1, 8):
+                    send(f"dag{k}", piece, piece, arm_dev(d))
+
+    def pass_on(k):
+        if TWO_LEVEL[k]:
+            (s0, n0), (s1, n1) = HALF[k]
+            arrived(f"first{k}", rxa[k].at[pl.ds(1, 2)])
+            for d in (1, 2, 3):
+                piece = dens.at[x, ys[d], pl.ds(s0, n0)]
+                send(f"dag{k}", piece, piece, arm_dev(4))
+            piece = dens.at[ox, y, pl.ds(s1, n1)]
+            for d in (1, 2, 3):
                 send(f"dag{k}", piece, piece, arm_dev(d))
 
     loaded(4, par, pv)
@@ -338,7 +358,9 @@
     for k in range(NC):
         gather_density(k)
     for k in range(NC):
-        arrived(f"dag{k}", rxa[k].at[pl.ds(1, 7)])
+        pass_on(k)
+    for k in range(NC):
+        arrived(f"dag{k}", rxa[k].at[pl.ds(1, 5 if TWO_LEVEL[k] else 7)])
     for group, like in sizes:
         pltpu.make_async_copy(like, like, ssem.at[groups[group]]).wait()
 

time: 60.9 us -> 57.8 us (0.949)
  Pallas kernels: 56.9 us -> 53.7 us
    pallas_call x1, Pallas kernels: 56.9 us -> 53.7 us  [local(): pl.pallas_call(kernel, name='star', out_shape=[jax.ShapeDtypeStruct(forwa...]
where the time goes in v4:
time: 57.8 us; the launch traced here: 57.6 us
  Pallas kernels  53.7 us (93%)
  local copies, waits for them, and re-layouts  3.25 us (6%)
  between operations  0.65 us (1%)
    pallas_call x1, Pallas kernels, local(): pl.pallas_call(kernel, name='star', out_shape=[jax.ShapeDtypeStruct(forwa...  53.7 us
    unnamed x6, local copies, waits for them, and re-layouts  3.25 us

profile of v4, /device:TPU:2, one launch (start us, length us, event | category | flops | bytes accessed | tf_op | source)
XLA Modules:
  0.0 57.6 jit_solution(5082996615459820933)
XLA Ops:
  0.6 0.0 copy-start
  0.6 0.6 %copy-done = s32[2]{0:T(128)S(1)} copy-done((s32[2]{0:T(128)S(1)}, s32[2]{0:T(128)}, u32[]{:S(2)}) %copy-start) | copy-done | bytes 32
  1.3 0.0 copy-start.1
  1.3 0.7 %copy-done.1 = s32[2]{0:T(128)S(1)} copy-done((s32[2]{0:T(128)S(1)}, s32[2]{0:T(128)}, u32[]{:S(2)}) %copy-start.1) | copy-done | bytes 32
  1.9 53.7 %star.1 = (f32[2,4,128,256]{3,2,1,0:T(8,128)S(1)}, f32[2,4,128,256]{3,2,1,0:T(8,128)S(1)}) custom-call(s32[2]{0:T(128)S(1)} %copy-done, s32[2]{0:T(128)S(1)} %copy-done.1, f32[2,4,128,256]{3,2,1,0:T(8,128)} %fwd.1, f32[2,4,128,256]{3,2,1,0:T(8,128)} %par.1, f32[2,4,128,256]{3,2,1,0:T(8,128)} %pot.1), custom_call_target="tpu_custom_call" | custom-call | flops 20000000 | bytes 5242880 | tf_op jit(solution)/shard_map/star/pallas_call | solution.py:377
  55.7 1.0 %copy.9 = f32[2,4,128,256]{3,2,1,0:T(8,128)} copy(f32[2,4,128,256]{3,2,1,0:T(8,128)S(1)} %get-tuple-element.4) | data formatting | bytes 2097152
  56.7 1.0 %copy.10 = f32[2,4,128,256]{3,2,1,0:T(8,128)} copy(f32[2,4,128,256]{3,2,1,0:T(8,128)S(1)} %get-tuple-element.5) | data formatting | bytes 2097152
Async XLA Ops:
  0.6 0.7 %copy-start = (s32[2]{0:T(128)S(1)}, s32[2]{0:T(128)}, u32[]{:S(2)}) copy-start(s32[2]{0:T(128)} %lab_h.1) | copy-start | bytes 28
  1.3 0.7 %copy-start.1 = (s32[2]{0:T(128)S(1)}, s32[2]{0:T(128)}, u32[]{:S(2)}) copy-start(s32[2]{0:T(128)} %len_h.1) | copy-start | bytes 28

commit v5 on v4

--- a/solution.py
+++ b/solution.py
@@ -47,7 +47,7 @@
     return slice(h * LANES, (h + 1) * LANES)
 
 
-def kernel(lab_h, len_h, fwd, par, pot, conj, dens, *scratch):
+def kernel(label_length, fwd, par, pot, conj, dens, *scratch):
     scratch = list(scratch)
 
     def take(n):
@@ -55,7 +55,7 @@
         del scratch[:n]
         return out
 
-    lab, length, fv, pv, uv, ifac, es, ce, pes, pe, gp, v1, v2, v3 = take(14)
+    scalars, fv, pv, uv, ifac, es, ce, pes, pe, gp, v1, v2, v3 = take(13)
     p, prx, pxx, pf, g, q = (take(NC) for _ in range(6))
     da, rxa = (take(NC) for _ in range(2))
     lsem, ssem, rsem = take(3)
@@ -75,7 +75,7 @@
     quarters = [pl.ds(r, 1) for r in range(ROWS)]
     for r in quarters:
         pltpu.make_async_copy(fwd.at[:, r], fv.at[:, r], lsem.at[0]).start()
-    for i, (src, dst) in enumerate(((pot, uv), (lab_h, lab), (len_h, length), (par, pv))):
+    for i, (src, dst) in enumerate(((pot, uv), (label_length, scalars), (par, pv))):
         pltpu.make_async_copy(src, dst, lsem.at[i + 1]).start()
 
     def loaded(i, src, dst):
@@ -211,9 +211,8 @@
     scatter(0)
     scatter(2)
     loaded(1, pot, uv)
-    loaded(2, lab_h, lab)
-    loaded(3, len_h, length)
-    l = [lab[a] == 1 for a in range(2)]
+    loaded(2, label_length, scalars)
+    l = [scalars[a] == 1 for a in range(2)]
     work_out(0)
     coefficients(0)
     work_out(2)
@@ -278,7 +277,7 @@
                             gp[side, r, a, h, 6 * side:6 * side + 2] = ce[side, r, j:j + 2]
 
         for t, (src, dst) in enumerate(((v1, v2), (v2, v3))):
-            act = [length[a] > t for a in range(2)]
+            act = [scalars[2 + a] > t for a in range(2)]
 
             @pl.loop(1 + t, 9 - t)
             def _(r):
@@ -289,7 +288,7 @@
                         for h in range(2):
                             dst[a, r, h, b:b + 8] = out[h]
 
-        act = [length[a] > 2 for a in range(2)]
+        act = [scalars[2 + a] > 2 for a in range(2)]
         for i in (1, 2, 3, 0):
             r = ys[i]
             for half in range(2):
@@ -352,7 +351,7 @@
             for d in (1, 2, 3):
                 send(f"dag{k}", piece, piece, arm_dev(d))
 
-    loaded(4, par, pv)
+    loaded(3, par, pv)
     for k in range(NC):
         steps(k)
     for k in range(NC):
@@ -378,10 +377,10 @@
         kernel,
         name="star",
         out_shape=[jax.ShapeDtypeStruct(forward_end.shape, F32), jax.ShapeDtypeStruct(potential.shape, F32)],
-        in_specs=[pl.BlockSpec(memory_space=pl.ANY)] * 5,
+        in_specs=[pl.BlockSpec(memory_space=pl.ANY)] * 4,
         out_specs=[pl.BlockSpec(memory_space=pltpu.VMEM)] * 2,
         scratch_shapes=[
-            pltpu.SMEM((2,), jnp.int32), pltpu.SMEM((2,), jnp.int32), full, full, full, full,
+            pltpu.SMEM((4,), jnp.int32), full, full, full, full,
             v(2, ROWS, 24, LANES), v(2, 10, 24, LANES), v(2, ROWS, 8, LANES), v(2, 10, 8, LANES),
             v(2, 10, 2, 2, 8, LANES),
             v(2, 10, 2, YD, LANES), v(2, 10, 2, YD, LANES), v(2, 10, 2, YD, LANES),
@@ -394,10 +393,10 @@
         + [v(10, 2, 2, n, LANES) for n in YC]
         + [v(2, ROWS, 2 * n, wide) for n in nh]
         + [v(8, 2 * n, wide) for n in nh]
-        + [dma((n,)) for n in (5, SEMS, SEMS)],
+        + [dma((n,)) for n in (4, SEMS, SEMS)],
         compiler_params=pltpu.CompilerParams(collective_id=0, has_side_effects=True, vmem_limit_bytes=51 << 20),
         cost_estimate=pl.CostEstimate(flops=20_000_000, bytes_accessed=5 << 20, transcendentals=1 << 19),
-    )(species_label, arm_length, forward_end, partner_end, potential)
+    )(jnp.concatenate([species_label, arm_length]), forward_end, partner_end, potential)
 
 
 def solution(mesh):

time: 57.8 us -> 57.2 us (0.990)
  local copies, waits for them, and re-layouts: 3.25 us -> 1.94 us
  other arithmetic: 0 us -> 0.75 us
    unnamed x6 -> x2, local copies, waits for them, and re-layouts: 3.25 us -> 1.94 us
    concatenate x0 -> x1, other arithmetic: none -> 0.75 us  [local(): jnp.concatenate([species_label, arm_length])]
where the time goes in v5:
time: 57.2 us; the launch traced here: 57 us
  Pallas kernels  53.7 us (94%)
  local copies, waits for them, and re-layouts  1.94 us (3%)
  other arithmetic  0.75 us (1%)
  between operations  0.64 us (1%)
    pallas_call x1, Pallas kernels, local(): pl.pallas_call(kernel, name='star', out_shape=[jax.ShapeDtypeStruct(forwa...  53.7 us
    unnamed x2, local copies, waits for them, and re-layouts  1.94 us

profile of v5, /device:TPU:2, one launch (start us, length us, event | category | flops | bytes accessed | tf_op | source)
XLA Modules:
  0.0 57.0 jit_solution(3204187039376615512)
XLA Ops:
  0.6 0.7 %pad_add_fusion.label_length = s32[4]{0:T(128)S(1)} fusion(s32[2]{0:T(128)} %param.9, s32[2]{0:T(128)} %param.8), kind=kLoop, calls=%fused_computation | loop fusion | flops 4 | bytes 32 | tf_op jit(solution)/shard_map/concatenate | solution.py:399
  1.4 53.7 %star.1 = (f32[2,4,128,256]{3,2,1,0:T(8,128)S(1)}, f32[2,4,128,256]{3,2,1,0:T(8,128)S(1)}) custom-call(s32[4]{0:T(128)S(1)} %pad_add_fusion.label_length, f32[2,4,128,256]{3,2,1,0:T(8,128)} %fwd.1, f32[2,4,128,256]{3,2,1,0:T(8,128)} %par.1, f32[2,4,128,256]{3,2,1,0:T(8,128)} %pot.1), custom_call_target="tpu_custom_call" | custom-call | flops 20000000 | bytes 5242880 | tf_op jit(solution)/shard_map/star/pallas_call | solution.py:376
  55.1 1.0 %copy.9 = f32[2,4,128,256]{3,2,1,0:T(8,128)} copy(f32[2,4,128,256]{3,2,1,0:T(8,128)S(1)} %get-tuple-element.4) | data formatting | bytes 2097152
  56.1 1.0 %copy.10 = f32[2,4,128,256]{3,2,1,0:T(8,128)} copy(f32[2,4,128,256]{3,2,1,0:T(8,128)S(1)} %get-tuple-element.5) | data formatting | bytes 2097152

commit v6 on v5

--- a/solution.py
+++ b/solution.py
@@ -279,7 +279,7 @@
         for t, (src, dst) in enumerate(((v1, v2), (v2, v3))):
             act = [scalars[2 + a] > t for a in range(2)]
 
-            @pl.loop(1 + t, 9 - t)
+            @pl.loop(1 + t, 9 - t, unroll=2)
             def _(r):
                 for tile in TILES[k]:
                     b = Y0 + 8 * tile

time: 57.2 us -> 56.7 us (level)
  no operation moved by 1% of the time
where the time goes in v6:
time: 56.7 us; the launch traced here: 56.6 us
  Pallas kernels  53.3 us (94%)
  local copies, waits for them, and re-layouts  1.94 us (3%)
  other arithmetic  0.75 us (1%)
  between operations  0.64 us (1%)
    pallas_call x1, Pallas kernels, local(): pl.pallas_call(kernel, name='star', out_shape=[jax.ShapeDtypeStruct(forwa...  53.3 us
    unnamed x2, local copies, waits for them, and re-layouts  1.94 us

profile of v6, /device:TPU:2, one launch (start us, length us, event | category | flops | bytes accessed | tf_op | source)
XLA Modules:
  0.0 56.6 jit_solution(13666445981986067869)
XLA Ops:
  0.6 0.7 %pad_add_fusion.label_length = s32[4]{0:T(128)S(1)} fusion(s32[2]{0:T(128)} %param.9, s32[2]{0:T(128)} %param.8), kind=kLoop, calls=%fused_computation | loop fusion | flops 4 | bytes 32 | tf_op jit(solution)/shard_map/concatenate | solution.py:399
  1.4 53.3 %star.1 = (f32[2,4,128,256]{3,2,1,0:T(8,128)S(1)}, f32[2,4,128,256]{3,2,1,0:T(8,128)S(1)}) custom-call(s32[4]{0:T(128)S(1)} %pad_add_fusion.label_length, f32[2,4,128,256]{3,2,1,0:T(8,128)} %fwd.1, f32[2,4,128,256]{3,2,1,0:T(8,128)} %par.1, f32[2,4,128,256]{3,2,1,0:T(8,128)} %pot.1), custom_call_target="tpu_custom_call" | custom-call | flops 20000000 | bytes 5242880 | tf_op jit(solution)/shard_map/star/pallas_call | solution.py:376
  54.7 1.0 %copy.9 = f32[2,4,128,256]{3,2,1,0:T(8,128)} copy(f32[2,4,128,256]{3,2,1,0:T(8,128)S(1)} %get-tuple-element.4) | data formatting | bytes 2097152
  55.6 1.0 %copy.10 = f32[2,4,128,256]{3,2,1,0:T(8,128)} copy(f32[2,4,128,256]{3,2,1,0:T(8,128)S(1)} %get-tuple-element.5) | data formatting | bytes 2097152
